TPU v7x, 32 devices: a whole 2x2x4 slice. The times are simulated.
32 devices in a mesh: tm: 32 (over z, y, x, core), band: 1, fsdp: 1.
Axes of the slice: x: 2, y: 2, z: 4, core: 2. Of those that a mesh axis runs over, the one named last changes fastest.
Arguments:
- video: bfloat16 [128, 16, 32, 256], P('tm', 'band', 'fsdp'), may hold values from -8 to 8
- clip_lengths: int32 [16], replicated, may hold values from 1 to 31, 128 in all
- norm_gains: float32 [2, 256], replicated, may hold values from 0.1 to 1.9
- spatial_kernel_weight: bfloat16 [256, 2304], P(('band', 'fsdp')), may hold values from -0.125 to 0.125
- w_time: bfloat16 [256, 768], P(('band', 'fsdp')), may hold values from -0.21875 to 0.21875
- w_qkv: bfloat16 [256, 768], P(('band', 'fsdp')), may hold values from -4 to 4
- w_out: bfloat16 [256, 256], P(('band', 'fsdp')), may hold values from -0.375 to 0.375
Outputs:
- mixed: bfloat16 [1, 1, 512, 128, 256], P('band', 'fsdp', 'tm')
Inputs may be any that keep to these rules, and one draw needn't show every extreme that they name: `clip_lengths`: every clip has at least one frame and the lengths sum to 128.
All inputs are finite; a program needn't handle non-finite values.
Results may differ from a plain program's by a relative error of at most 0.0064.
Values may be sent and summed in bfloat16 or wider, within the bound.
A program may use at most 64 MiB of HBM per device.

v0:
```python
import math

import jax
import jax.numpy as jnp
from jax import lax
from jax.sharding import PartitionSpec as P

GROUPS = 32


EPS = 1e-06


def with_halo(x, sides, width):
    for axis, dim in sides:
        size, length = (lax.axis_size(axis), x.shape[dim])
        up = [(i, (i + 1) % size) for i in range(size - 1)]
        down = [(j, i) for i, j in up]
        last = lax.slice_in_dim(x, length - width, length, axis=dim)
        initial = lax.slice_in_dim(x, 0, width, axis=dim)
        before = lax.ppermute(last, axis, up)
        after = lax.ppermute(initial, axis, down)
        x = jnp.concatenate([before, x, after], axis=dim)
    return x


def from_behind(x, axis, by):
    length = lax.axis_size(axis)
    pairs = [(i, i + by) for i in range(length) if 0 <= i + by < length]
    return lax.ppermute(x, axis, pairs)


def frame_starts(clip_lengths, total):
    ends = jnp.cumsum(clip_lengths)
    begins = ends - clip_lengths
    index = jnp.arange(total, dtype=jnp.int32)
    chosen = jnp.where(begins[None, :] <= index[:, None], begins[None, :], 0)
    return jnp.max(chosen, axis=1)


def group_moments(field):
    frames, height, width, chans = field.shape
    group_width = chans // GROUPS
    vals = field.astype(jnp.float32).reshape(frames, height * width, GROUPS, group_width)
    sums = jnp.sum(vals, axis=(1, 3))
    squares = jnp.sum(vals * vals, axis=(1, 3))
    sums, squares = lax.psum((sums, squares), ("band", "fsdp"))
    count = height * width * group_width * lax.axis_size("band") * lax.axis_size("fsdp")
    mean = sums / count
    scale = lax.rsqrt(squares / count - mean * mean + EPS)
    return (mean, scale)


def apply_norm(field, mean, scale, gain):
    shape = field.shape
    chans = shape[-1]
    group_width = chans // GROUPS
    vals = field.astype(jnp.float32).reshape(shape[0], -1, GROUPS, group_width)
    normed = (vals - mean[:, None, :, None]) * scale[:, None, :, None]
    return normed.reshape(shape) * gain


def body(video, clip_lengths, norm_gains, spatial_kernel_weight, w_time, w_qkv, w_out):
    space_full, time_full, qkv_full, output_complete = (
        lax.all_gather(spatial_kernel_weight, ("band", "fsdp"), axis=0, tiled=True),
        lax.all_gather(w_time, ("band", "fsdp"), axis=0, tiled=True),
        lax.all_gather(w_qkv, ("band", "fsdp"), axis=0, tiled=True),
        lax.all_gather(w_out, ("band", "fsdp"), axis=0, tiled=True),
    )
    frames, height, width, chans = video.shape
    ranks = lax.axis_size("tm")
    total_frames = frames * ranks
    first = lax.axis_index("tm") * frames
    starts = frame_starts(clip_lengths, total_frames)
    local_starts = lax.dynamic_slice_in_dim(starts, first, frames)
    mean_one, scale_one = group_moments(video)
    act = jax.nn.silu(apply_norm(video, mean_one, scale_one, norm_gains[0])).astype(jnp.bfloat16)
    padded = with_halo(act, (("band", 1), ("fsdp", 2)), 1)
    spatial = jnp.zeros((frames, height, width, chans), jnp.float32)
    for tap in range(9):
        shift_y = tap // 3
        shift_x = tap % 3
        spatial = spatial + jnp.einsum(
            "fhwc,cd->fhwd",
            padded[:, shift_y : shift_y + height, shift_x : shift_x + width],
            space_full[:, tap * chans : (tap + 1) * chans],
            preferred_element_type=jnp.float32,
        )
    spatial = spatial.astype(jnp.bfloat16)
    carried = from_behind(spatial[frames - 2 :], "tm", 1)
    extended = jnp.concatenate([carried, spatial], axis=0)
    position = first + jnp.arange(frames, dtype=jnp.int32)
    slots = jnp.arange(frames + 2, dtype=jnp.int32)
    temporal = jnp.zeros((frames, height, width, chans), jnp.float32)
    for tap in range(3):
        source = jnp.maximum(position - 2 + tap, local_starts) - first + 2
        select = (source[:, None] == slots[None, :]).astype(jnp.bfloat16)
        picked = jnp.einsum(
            "fe,ehwc->fhwc", select, extended, preferred_element_type=jnp.float32
        ).astype(jnp.bfloat16)
        temporal = temporal + jnp.einsum(
            "fhwc,cd->fhwd",
            picked,
            time_full[:, tap * chans : (tap + 1) * chans],
            preferred_element_type=jnp.float32,
        )
    resid = (video.astype(jnp.float32) + temporal).astype(jnp.bfloat16)
    mean_two, scale_two = group_moments(resid)
    pixels = height * width
    flat_resid = resid.reshape(frames, pixels, chans)
    flat_norm = (
        apply_norm(resid, mean_two, scale_two, norm_gains[1])
        .astype(jnp.bfloat16)
        .reshape(frames, pixels, chans)
    )
    qkv = jnp.einsum("fpc,cd->fpd", flat_norm, qkv_full, preferred_element_type=jnp.float32).astype(
        jnp.bfloat16
    )
    qkv_time, resid_time = (
        lax.all_to_all(qkv, "tm", split_axis=1, concat_axis=0, tiled=True),
        lax.all_to_all(flat_resid, "tm", split_axis=1, concat_axis=0, tiled=True),
    )
    query = qkv_time[..., :chans]
    keys = qkv_time[..., chans : 2 * chans]
    value_rows = qkv_time[..., 2 * chans :]
    index = jnp.arange(total_frames, dtype=jnp.int32)
    allowed = (index[None, :] <= index[:, None]) & (index[None, :] >= starts[:, None])
    scores = jnp.einsum(
        "fpc,gpc->pfg", query, keys, preferred_element_type=jnp.float32
    ) / math.sqrt(chans)
    scores = jnp.where(allowed[None], scores, -1e30)
    top = jnp.max(scores, axis=-1, keepdims=True)
    expo = jnp.where(allowed[None], jnp.exp(scores - top), 0.0)
    attention_probabilities = (expo / jnp.sum(expo, axis=-1, keepdims=True)).astype(jnp.bfloat16)
    attention_output = jnp.einsum(
        "boh,hba->boa", attention_probabilities, value_rows, preferred_element_type=jnp.float32
    ).astype(jnp.bfloat16)
    projected_output = jnp.einsum(
        "axi,iy->axy", attention_output, output_complete, preferred_element_type=jnp.float32
    )
    mixed = (jnp.swapaxes(resid_time, 0, 1).astype(jnp.float32) + projected_output).astype(
        jnp.bfloat16
    )
    return mixed.reshape(1, 1, mixed.shape[0], total_frames, chans)


def solution(mesh):
    return jax.shard_map(
        body,
        mesh=mesh,
        in_specs=(
            P("tm", "band", "fsdp", None),
            P(),
            P(),
            P(("band", "fsdp"), None),
            P(("band", "fsdp"), None),
            P(("band", "fsdp"), None),
            P(("band", "fsdp"), None),
        ),
        out_specs=P("band", "fsdp", "tm", None, None),
        check_vma=False,
    )
```

profile of v0, /device:TPU:0, one launch (start us, length us, event | category | flops | bytes accessed | tf_op | source)
XLA Modules:
  0.0 154.1 jit_solution(4117776689518994071)
XLA Ops:
  0.0 1.7 %convert_reduce_fusion = (f32[4,256]{1,0:T(4,128)S(1)}, f32[4,256]{1,0:T(4,128)S(1)}) fusion(bf16[4,16,32,256]{3,2,1,0:T(8,128)(2,1)} %param.7), kind=kLoop, calls=%fused_computation.4 | loop fusion | flops 2095104 | bytes 1056768 | tf_op jit(solution)/shard_map/reduce_sum | solution.py:45
  2.5 1.4 fusion.109
  3.8 0.7 fusion.18
  4.5 0.7 collective-permute-start
  5.2 0.7 collective-permute-start.1
  6.4 0.7 collective-permute-start.2
  7.1 0.7 collective-permute-start.3
  8.6 0.9 pad_maximum_fusion.1
  10.4 0.5 fusion.54
  10.9 0.5 fusion.58
  11.8 2.0 %add_convert_fusion = bf16[4,16,32,256]{3,2,1,0:T(8,128)(2,1)S(1)} fusion(f32[4,16,32,256]{3,2,1,0:T(8,128)S(1)} %fusion.40, f32[4,16,32,256]{3,2,1,0:T(8,128)S(1)} %fusion.52, f32[4,16,32,256]{3,2,1,0:T(8,128)S(1)} %fusion.54, f32[4,16,32,256]{3,2,1,0:T(8,128)S(1)} %fusion.77, f32[4,16,32,256]{3,2,1,0:T(8,128)S(1)} %fusion.56, ...), kind=kOutput, calls=%fused_computation.33 | convolution fusion | flops 273154048 | bytes 19005440 | tf_op jit(solution)/shard_map/fhwc,cd->fhwd/dot_general | solution.py:83
  13.8 2.6 %collective-permute-start.4 = (bf16[2,16,32,256]{3,2,1,0:T(8,128)(2,1)S(1)}, bf16[2,16,32,256]{3,2,1,0:T(8,128)(2,1)S(1)}, u32[]{:S(2)}, u32[]{:S(2)}) collective-permute-start(bf16[2,16,32,256]{3,2,1,0:T(8,128)(2,1)S(1)} %slice.136), channel_id=1, source_target_pairs={{0,1},{1,2},{2,3},{3,4},{4,5},{5,6},{6,7},{7,8},{8,9},{9,10},{10,1... | collective-permute-start | bytes 1572872 | tf_op jit(solution)/shard_map/ppermute | solution.py:30
  16.7 0.7 sub.69
  18.1 1.2 fusion.25
  19.3 1.2 fusion.22
  20.9 0.4 fusion.65
  21.4 1.2 fusion.28
  22.6 0.9 convert_reduce_fusion.1
  23.5 1.8 %copy.33 = bf16[4,512,256]{2,0,1:T(4,128)(2,1)} copy(bf16[4,512,256]{2,1,0:T(8,128)(2,1)S(1)} %bitcast.112) | data formatting | bytes 2097152 | tf_op jit(solution)/shard_map/reshape | solution.py:110
  25.3 13.8 %all-to-all-start = ((bf16[4,512,256]{2,0,1:T(4,128)(2,1)}), bf16[4,512,256]{2,0,1:T(4,128)(2,1)}, u32[]{:S(2)}, u32[]{:S(2)}) async-start(bf16[4,512,256]{2,0,1:T(4,128)(2,1)} %copy.33), calls=%async_computation | async-start | bytes 2097152 | tf_op jit(solution)/shard_map/all_to_all | solution.py:121
  40.3 1.0 convolution_convert_fusion
  41.2 4.1 %copy.35 = bf16[4,512,768]{2,0,1:T(4,128)(2,1)} copy(bf16[4,512,768]{2,1,0:T(8,128)(2,1)S(1)} %convolution_convert_fusion) | data formatting | bytes 6291456 | tf_op jit(solution)/shard_map/convert_element_type | solution.py:116
  45.3 20.0 %all-to-all-done = bf16[4,512,256]{2,0,1:T(4,128)(2,1)} async-done(((bf16[4,512,256]{2,0,1:T(4,128)(2,1)}), bf16[4,512,256]{2,0,1:T(4,128)(2,1)}, u32[]{:S(2)}, u32[]{:S(2)}) %all-to-all-start) | async-done | bytes 1048608 | tf_op jit(solution)/shard_map/all_to_all | solution.py:121
  65.3 3.8 %all-to-all-start.1 = ((bf16[4,512,768]{2,0,1:T(4,128)(2,1)}), bf16[4,512,768]{2,0,1:T(4,128)(2,1)S(1)}, u32[]{:S(2)}, u32[]{:S(2)}) async-start(bf16[4,512,768]{2,0,1:T(4,128)(2,1)} %copy.35), calls=%async_computation.1 | async-start | bytes 6291456 | tf_op jit(solution)/shard_map/all_to_all | solution.py:120
  69.2 0.6 fusion.96
  69.8 3.2 %copy_bitcast_fusion.1 = f32[32,4,16,256]{3,1,0,2:T(4,128)} fusion(bf16[4,32,16,256]{3,0,2,1:T(4,128)(2,1)} %bitcast.58), kind=kLoop, calls=%fused_computation.32 | loop fusion | flops 524288 | bytes 3145728 | tf_op jit(solution)/shard_map/convert_element_type | solution.py:141
  73.0 3.0 %reshape.121 = f32[128,16,256]{2,0,1:T(8,128)} reshape(f32[32,4,16,256]{3,1,0,2:T(4,128)} %copy_bitcast_fusion.1) | data formatting | bytes 4194304 | tf_op jit(solution)/shard_map/convert_element_type | solution.py:141
  75.9 64.6 %all-to-all-done.1 = bf16[4,512,768]{2,0,1:T(4,128)(2,1)S(1)} async-done(((bf16[4,512,768]{2,0,1:T(4,128)(2,1)}), bf16[4,512,768]{2,0,1:T(4,128)(2,1)S(1)}, u32[]{:S(2)}, u32[]{:S(2)}) %all-to-all-start.1) | async-done | bytes 3145760 | tf_op jit(solution)/shard_map/all_to_all | solution.py:120
  140.5 3.2 %copy.76 = bf16[4,32,16,768]{3,0,1,2:T(4,128)(2,1)} copy(bf16[4,32,16,768]{3,0,2,1:T(4,128)(2,1)S(1)} %bitcast.110) | data formatting | bytes 6291456 | tf_op jit(solution)/shard_map/all_to_all | solution.py:120
  143.7 4.5 %all_to_all.24 = bf16[128,16,768]{2,0,1:T(8,128)(2,1)S(1)} reshape(bf16[32,4,16,768]{3,1,0,2:T(4,128)(2,1)} %bitcast.111) | data formatting | bytes 6291456 | tf_op jit(solution)/shard_map/all_to_all | solution.py:120
  148.2 2.1 %fusion.110 = (f32[16,128]{1,0:T(8,128)}, f32[16,128,128]{1,2,0:T(8,128)}) fusion(pred[128,128]{0,1:T(8,128)(4,1)S(1)} %fusion.96, bf16[128,16,768]{2,0,1:T(8,128)(2,1)S(1)} %all_to_all.24), kind=kOutput, calls=%fused_computation.133 | convolution fusion | flops 135528576 | bytes 3186688 | tf_op jit(solution)/shard_map/sub | solution.py:133
  150.3 3.7 %fusion.34 = bf16[1,1,16,128,256]{4,3,2,1,0:T(8,128)(2,1)} fusion(f32[128,16,256]{2,0,1:T(8,128)} %reshape.121, bf16[128,16,768]{2,0,1:T(8,128)(2,1)S(1)} %all_to_all.24, f32[16,128,128]{1,2,0:T(8,128)} %get-tuple-element.26, f32[16,128]{1,0:T(8,128)} %get-tuple-element.25, bf16[256,256]{1,0:T(8,128)(2,1)} %param.13), kind=kOutput, calls=%fused_computation.44 | convolution fusion | flops 404750336 | bytes 5382144 | tf_op jit(solution)/shard_map/axi,iy->axy/dot_general | solution.py:138
  (54 shorter events, 6.0 us)
Async XLA Ops:
  0.0 40.2 %copy-start = (bf16[256,768]{1,0:T(8,128)(2,1)S(1)}, bf16[256,768]{1,0:T(8,128)(2,1)}, u32[]{:S(2)}) copy-start(bf16[256,768]{1,0:T(8,128)(2,1)} %param.12) | copy-start | bytes 1179652
  0.0 3.8 %copy-start.1 = (bf16[4,16,32,256]{3,2,1,0:T(8,128)(2,1)S(1)}, bf16[4,16,32,256]{3,2,1,0:T(8,128)(2,1)}, u32[]{:S(2)}) copy-start(bf16[4,16,32,256]{3,2,1,0:T(8,128)(2,1)} %param.7) | copy-start | bytes 3145732
  0.0 5.8 %copy-start.2 = (bf16[256,2304]{1,0:T(8,128)(2,1)S(1)}, bf16[256,2304]{1,0:T(8,128)(2,1)}, u32[]{:S(2)}) copy-start(bf16[256,2304]{1,0:T(8,128)(2,1)} %param.10) | copy-start | bytes 3538948
  4.5 1.8 %collective-permute-start = (bf16[4,1,32,256]{3,2,1,0:T(8,128)(2,1)S(1)}, bf16[4,1,32,256]{3,2,1,0:T(8,128)(2,1)S(1)}, u32[]{:S(2)}, u32[]{:S(2)}) collective-permute-start(bf16[4,1,32,256]{3,2,1,0:T(8,128)(2,1)S(1)} %get-tuple-element.13), channel_id=1, source_target_pairs={} | collective-permute-start | bytes 196616 | tf_op jit(solution)/shard_map/ppermute | solution.py:21
  5.2 1.1 collective-permute-start.1
  6.4 2.2 %collective-permute-start.2 = (bf16[4,18,1,256]{3,2,1,0:T(2,128)(2,1)S(1)}, bf16[4,18,1,256]{3,2,1,0:T(2,128)(2,1)S(1)}, u32[]{:S(2)}, u32[]{:S(2)}) collective-permute-start(bf16[4,18,1,256]{3,2,1,0:T(2,128)(2,1)S(1)} %get-tuple-element.12), channel_id=1, source_target_pairs={} | collective-permute-start | bytes 110600 | tf_op jit(solution)/shard_map/ppermute | solution.py:21
  7.1 1.5 collective-permute-start.3
  11.8 4.6 %copy-start.6 = (s32[16]{0:T(128)S(1)}, s32[16]{0:T(128)}, u32[]{:S(2)}) copy-start(s32[16]{0:T(128)} %param.8) | copy-start | bytes 196
  13.8 4.1 %collective-permute-start.4 = (bf16[2,16,32,256]{3,2,1,0:T(8,128)(2,1)S(1)}, bf16[2,16,32,256]{3,2,1,0:T(8,128)(2,1)S(1)}, u32[]{:S(2)}, u32[]{:S(2)}) collective-permute-start(bf16[2,16,32,256]{3,2,1,0:T(8,128)(2,1)S(1)} %slice.136), channel_id=1, source_target_pairs={{0,1},{1,2},{2,3},{3,4},{4,5},{5,6},{6,7},{7,8},{8,9},{9,10},{10,1... | collective-permute-start | bytes 1572872 | tf_op jit(solution)/shard_map/ppermute | solution.py:30
  17.4 0.5 copy-start.5
  19.3 1.2 copy-start.3
  23.5 16.4 %copy-start.4 = (f32[1,256]{1,0:T(1,128)S(1)}, f32[1,256]{1,0:T(1,128)}, u32[]{:S(2)}) copy-start(f32[1,256]{1,0:T(1,128)} %get-tuple-element.17) | copy-start | bytes 3076
  25.3 40.0 %all-to-all-start = ((bf16[4,512,256]{2,0,1:T(4,128)(2,1)}), bf16[4,512,256]{2,0,1:T(4,128)(2,1)}, u32[]{:S(2)}, u32[]{:S(2)}) async-start(bf16[4,512,256]{2,0,1:T(4,128)(2,1)} %copy.33), calls=%async_computation | async-start | bytes 2097152 | tf_op jit(solution)/shard_map/all_to_all | solution.py:121
  65.3 75.2 %all-to-all-start.1 = ((bf16[4,512,768]{2,0,1:T(4,128)(2,1)}), bf16[4,512,768]{2,0,1:T(4,128)(2,1)S(1)}, u32[]{:S(2)}, u32[]{:S(2)}) async-start(bf16[4,512,768]{2,0,1:T(4,128)(2,1)} %copy.35), calls=%async_computation.1 | async-start | bytes 6291456 | tf_op jit(solution)/shard_map/all_to_all | solution.py:120
where the time goes:
time: 155 us; the launch traced here: 154 us
  waiting for transfers between devices  84.6 us (55%)
  starting transfers between devices  22.9 us (15%)
  local copies, waits for them, and re-layouts  19.6 us (13%)
  matrix products  17.7 us (11%)
  other arithmetic  9 us (6%)
    all_to_all x1, waiting for transfers between devices, body(): lax.all_to_all(qkv, 'tm', split_axis=1, concat_axis=0, tiled=True)  64.6 us
    all_to_all x1, waiting for transfers between devices, body(): lax.all_to_all(flat_resid, 'tm', split_axis=1, concat_axis=0, tiled=True)  20 us
    all_to_all x1, starting transfers between devices, body(): lax.all_to_all(flat_resid, 'tm', split_axis=1, concat_axis=0, tiled=True)  13.8 us
    all_to_all x2, local copies, waits for them, and re-layouts, body(): lax.all_to_all(qkv, 'tm', split_axis=1, concat_axis=0, tiled=True)  7.7 us
    dot_general x9, matrix products, body(): jnp.einsum('fhwc,cd->fhwd', padded[:, shift_y:shift_y + height, shift_x:s...  5.49 us
    convert_element_type x1, local copies, waits for them, and re-layouts, body(): jnp.einsum('fpc,cd->fpd', flat_norm, qkv_full, preferred_element_type=jnp...  4.09 us
    all_to_all x1, starting transfers between devices, body(): lax.all_to_all(qkv, 'tm', split_axis=1, concat_axis=0, tiled=True)  3.84 us
    dot_general x1, matrix products, body(): jnp.einsum('axi,iy->axy', attention_output, output_complete, preferred_el...  3.71 us
  transfers between devices with their start and end apart: 7, of which 2 were waited for; matrix products, arithmetic and copies ran while one was open for 10% of the time, Pallas kernels for 0%

commit v1 on v0

--- a/solution.py
+++ b/solution.py
@@ -108,18 +108,15 @@
     mean_two, scale_two = group_moments(resid)
     pixels = height * width
     flat_resid = resid.reshape(frames, pixels, chans)
+    resid_time = lax.all_to_all(flat_resid, "tm", split_axis=1, concat_axis=0, tiled=True)
+    moments = lax.all_gather(jnp.stack([mean_two, scale_two]), "tm", axis=1, tiled=True)
+    wide = jnp.repeat(moments, chans // GROUPS, axis=2)
     flat_norm = (
-        apply_norm(resid, mean_two, scale_two, norm_gains[1])
-        .astype(jnp.bfloat16)
-        .reshape(frames, pixels, chans)
-    )
-    qkv = jnp.einsum("fpc,cd->fpd", flat_norm, qkv_full, preferred_element_type=jnp.float32).astype(
-        jnp.bfloat16
-    )
-    qkv_time, resid_time = (
-        lax.all_to_all(qkv, "tm", split_axis=1, concat_axis=0, tiled=True),
-        lax.all_to_all(flat_resid, "tm", split_axis=1, concat_axis=0, tiled=True),
-    )
+        (resid_time.astype(jnp.float32) - wide[0][:, None]) * wide[1][:, None] * norm_gains[1]
+    ).astype(jnp.bfloat16)
+    qkv_time = jnp.einsum(
+        "fpc,cd->fpd", flat_norm, qkv_full, preferred_element_type=jnp.float32
+    ).astype(jnp.bfloat16)
     query = qkv_time[..., :chans]
     keys = qkv_time[..., chans : 2 * chans]
     value_rows = qkv_time[..., 2 * chans :]

time: 155 us -> 107 us (0.69)
  waiting for transfers between devices: 84.6 us -> 0.02 us
  blocking collectives: 0 us -> 52.2 us
  local copies, waits for them, and re-layouts: 19.6 us -> 8.25 us
  starting transfers between devices: 22.9 us -> 18.8 us
  matrix products: 17.7 us -> 19.9 us
  other arithmetic: 9 us -> 6.81 us
    all_to_all x1 -> x0, waiting for transfers between devices: 64.6 us -> none  [body(): lax.all_to_all(qkv, 'tm', split_axis=1, concat_axis=0, tiled=True)]
    all_gather x0 -> x1, blocking collectives: none -> 52.2 us  [body(): lax.all_gather(jnp.stack([mean_two, scale_two]), 'tm', axis=1, tiled=True)]
    all_to_all x1, waiting for transfers between devices: 20 us -> 0.01 us  [body(): lax.all_to_all(flat_resid, 'tm', split_axis=1, concat_axis=0, tiled=True)]
    all_to_all x2 -> x0, local copies, waits for them, and re-layouts: 7.7 us -> none  [body(): lax.all_to_all(qkv, 'tm', split_axis=1, concat_axis=0, tiled=True)]
    convert_element_type x1 -> x0, local copies, waits for them, and re-layouts: 4.09 us -> none  [body(): jnp.einsum('fpc,cd->fpd', flat_norm, qkv_full, preferred_element_type=jnp...]
    all_to_all x1 -> x0, starting transfers between devices: 3.84 us -> none  [body(): lax.all_to_all(qkv, 'tm', split_axis=1, concat_axis=0, tiled=True)]
    dot_general x1, matrix products: 0.98 us -> 2.67 us  [body(): jnp.einsum('fpc,cd->fpd', flat_norm, qkv_full, preferred_element_type=jnp...]
    broadcast_in_dim x0 -> x4, local copies, waits for them, and re-layouts: none -> 1.55 us  [body(): wide = jnp.repeat(moments, chans // GROUPS, axis=2)]
  transfers between devices with their start and end apart: 7 -> 6, of which waited for: 2 -> 0; matrix products, arithmetic and copies ran while one was open for 10% -> 4% of each run, Pallas kernels for 0% -> 0%
where the time goes in v1:
time: 107 us; the launch traced here: 106 us
  blocking collectives  52.2 us (49%)
  matrix products  19.9 us (19%)
  starting transfers between devices  18.8 us (18%)
  local copies, waits for them, and re-layouts  8.25 us (8%)
  other arithmetic  6.81 us (6%)
    all_gather x1, blocking collectives, body(): lax.all_gather(jnp.stack([mean_two, scale_two]), 'tm', axis=1, tiled=True)  52.2 us
    all_to_all x1, starting transfers between devices, body(): lax.all_to_all(flat_resid, 'tm', split_axis=1, concat_axis=0, tiled=True)  13.6 us
    dot_general x9, matrix products, body(): jnp.einsum('fhwc,cd->fhwd', padded[:, shift_y:shift_y + height, shift_x:s...  5.49 us
    dot_general x3, matrix products, body(): jnp.einsum('fe,ehwc->fhwc', select, extended, preferred_element_type=jnp....  3.6 us
    dot_general x1, matrix products, body(): jnp.einsum('axi,iy->axy', attention_output, output_complete, preferred_el...  3.28 us
    sub x1, matrix products, body(): expo = jnp.where(allowed[None], jnp.exp(scores - top), 0.0)  3.13 us
    dot_general x1, matrix products, body(): jnp.einsum('fpc,cd->fpd', flat_norm, qkv_full, preferred_element_type=jnp...  2.67 us
    ppermute x1, starting transfers between devices, from_behind(): return lax.ppermute(x, axis, pairs)  2.58 us
  transfers between devices with their start and end apart: 6, of which 0 were waited for; matrix products, arithmetic and copies ran while one was open for 4% of the time, Pallas kernels for 0%

profile of v1, /device:TPU:0, one launch (start us, length us, event | category | flops | bytes accessed | tf_op | source)
XLA Modules:
  0.0 106.4 jit_solution(8221877811610722187)
XLA Ops:
  0.0 1.7 %convert_reduce_fusion = (f32[4,256]{1,0:T(4,128)S(1)}, f32[4,256]{1,0:T(4,128)S(1)}) fusion(bf16[4,16,32,256]{3,2,1,0:T(8,128)(2,1)} %param.7), kind=kLoop, calls=%fused_computation.4 | loop fusion | flops 2095104 | bytes 1056768 | tf_op jit(solution)/shard_map/reduce_sum | solution.py:45
  2.5 1.3 %fusion.112 = (f32[1,256]{1,0:T(1,128)}, f32[1,256]{1,0:T(1,128)S(1)}) fusion(f32[2,256]{1,0:T(2,128)} %param.9), kind=kLoop, calls=%fused_computation.137 | loop fusion | bytes 4096 | tf_op jit(solution)/shard_map/slice | solution.py:115
  3.7 0.7 fusion.15
  4.4 0.7 collective-permute-start
  5.1 0.7 collective-permute-start.1
  6.3 0.7 collective-permute-start.2
  7.0 0.7 collective-permute-start.3
  8.6 0.9 pad_maximum_fusion.1
  9.5 0.4 fusion.49
  9.9 0.4 fusion.53
  10.4 0.5 fusion.51
  10.8 0.5 fusion.55
  11.3 0.4 fusion.57
  11.7 2.0 %add_convert_fusion = bf16[4,16,32,256]{3,2,1,0:T(8,128)(2,1)S(1)} fusion(f32[4,16,32,256]{3,2,1,0:T(8,128)S(1)} %fusion.37, f32[4,16,32,256]{3,2,1,0:T(8,128)S(1)} %fusion.49, f32[4,16,32,256]{3,2,1,0:T(8,128)S(1)} %fusion.51, f32[4,16,32,256]{3,2,1,0:T(8,128)S(1)} %fusion.77, f32[4,16,32,256]{3,2,1,0:T(8,128)S(1)} %fusion.53, ...), kind=kOutput, calls=%fused_computation.29 | convolution fusion | flops 273154048 | bytes 19005440 | tf_op jit(solution)/shard_map/fhwc,cd->fhwd/dot_general | solution.py:83
  13.8 2.6 %collective-permute-start.4 = (bf16[2,16,32,256]{3,2,1,0:T(8,128)(2,1)S(1)}, bf16[2,16,32,256]{3,2,1,0:T(8,128)(2,1)S(1)}, u32[]{:S(2)}, u32[]{:S(2)}) collective-permute-start(bf16[2,16,32,256]{3,2,1,0:T(8,128)(2,1)S(1)} %slice.154), channel_id=1, source_target_pairs={{0,1},{1,2},{2,3},{3,4},{4,5},{5,6},{6,7},{7,8},{8,9},{9,10},{10,1... | collective-permute-start | bytes 1572872 | tf_op jit(solution)/shard_map/ppermute | solution.py:30
  16.6 0.7 sub.67
  17.4 0.5 copy-done.7
  18.1 1.2 %fusion.22 = bf16[4,16,32,256]{3,0,2,1:T(4,128)(2,1)S(1)} fusion(bf16[6,16,32,256]{3,2,1,0:T(8,128)(2,1)S(1)} %pad_maximum_fusion, s32[4]{0:T(128)S(1)} %get-tuple-element.23), kind=kOutput, calls=%fused_computation.32 | convolution fusion | flops 6815768 | bytes 2621456 | tf_op jit(solution)/shard_map/fe,ehwc->fhwc/dot_general | solution.py:98
  19.3 1.2 %fusion.19 = bf16[4,16,32,256]{3,0,2,1:T(4,128)(2,1)S(1)} fusion(bf16[6,16,32,256]{3,2,1,0:T(8,128)(2,1)S(1)} %pad_maximum_fusion, s32[4]{0:T(128)S(1)} %get-tuple-element.22), kind=kOutput, calls=%fused_computation.31 | convolution fusion | flops 6815768 | bytes 2621456 | tf_op jit(solution)/shard_map/fe,ehwc->fhwc/dot_general | solution.py:98
  20.9 0.4 fusion.62
  21.4 1.2 %fusion.25 = bf16[4,16,32,256]{3,0,2,1:T(4,128)(2,1)S(1)} fusion(bf16[6,16,32,256]{3,2,1,0:T(8,128)(2,1)S(1)} %pad_maximum_fusion, s32[4]{0:T(128)S(1)} %get-tuple-element.21), kind=kOutput, calls=%fused_computation.33 | convolution fusion | flops 6815768 | bytes 2621456 | tf_op jit(solution)/shard_map/fe,ehwc->fhwc/dot_general | solution.py:98
  22.6 0.9 convert_reduce_fusion.1
  23.5 1.8 %copy.38 = bf16[4,512,256]{2,0,1:T(4,128)(2,1)} copy(bf16[4,512,256]{2,1,0:T(8,128)(2,1)S(1)} %bitcast.119) | data formatting | bytes 2097152 | tf_op jit(solution)/shard_map/reshape | solution.py:110
  25.3 13.6 %all-to-all-start = ((bf16[4,512,256]{2,0,1:T(4,128)(2,1)}), bf16[4,512,256]{2,0,1:T(4,128)(2,1)S(1)}, u32[]{:S(2)}, u32[]{:S(2)}) async-start(bf16[4,512,256]{2,0,1:T(4,128)(2,1)} %copy.38), calls=%async_computation | async-start | bytes 2097152 | tf_op jit(solution)/shard_map/all_to_all | solution.py:111
  39.4 52.2 %all_gather.2 = f32[2,128,32]{2,0,1:T(2,128)S(1)} all-gather(f32[2,4,32]{2,0,1:T(2,128)S(1)} %copy.40), channel_id=1, replica_groups=mesh['tm'=32,'band'=1,'fsdp'=1] {'tm'}, dimensions={1}, use_global_device_ids=true | all-gather | bytes 33792 | tf_op jit(solution)/shard_map/all_gather | solution.py:112
  91.8 0.7 copy.42
  92.6 0.8 copy.44
  93.4 1.9 %copy_bitcast_fusion = f32[32,4,16,256]{3,1,0,2:T(4,128)} fusion(bf16[4,32,16,256]{3,0,2,1:T(4,128)(2,1)S(1)} %bitcast.118), kind=kLoop, calls=%fused_computation.27 | loop fusion | flops 524288 | bytes 3145728 | tf_op jit(solution)/shard_map/convert_element_type | solution.py:138
  95.3 2.0 %reshape.151 = f32[128,16,256]{2,0,1:T(8,128)S(1)} reshape(f32[32,4,16,256]{3,1,0,2:T(4,128)} %copy_bitcast_fusion) | data formatting | bytes 4194304 | tf_op jit(solution)/shard_map/convert_element_type | solution.py:138
  97.3 2.7 %convolution_convert_fusion = bf16[128,16,768]{2,0,1:T(8,128)(2,1)} fusion(f32[128,16,256]{2,0,1:T(8,128)S(1)} %reshape.151, f32[256]{0:T(256)S(1)} %bitcast.122, f32[128,256]{1,0:T(8,128)S(1)} %copy-done.4, f32[128,256]{1,0:T(8,128)S(1)} %copy-done.3, bf16[256,768]{1,0:T(8,128)(2,1)S(1)} %copy-done), kind=kOutput, calls=%fused_computation.7 | convolution fusion | flops 808976384 | bytes 5899264 | tf_op jit(solution)/shard_map/fpc,cd->fpd/dot_general | solution.py:117
  100.0 3.1 %fusion.113 = (f32[16,128]{1,0:T(8,128)S(1)}, f32[16,128,128]{1,2,0:T(8,128)}) fusion(pred[128,128]{0,1:T(8,128)(4,1)S(1)} %fusion.96, bf16[128,16,768]{2,0,1:T(8,128)(2,1)} %convolution_convert_fusion), kind=kOutput, calls=%fused_computation.138 | convolution fusion | flops 135528576 | bytes 3186688 | tf_op jit(solution)/shard_map/sub | solution.py:130
  103.2 3.3 %fusion.31 = bf16[1,1,16,128,256]{4,3,2,1,0:T(8,128)(2,1)} fusion(f32[128,16,256]{2,0,1:T(8,128)S(1)} %reshape.151, bf16[128,16,768]{2,0,1:T(8,128)(2,1)} %convolution_convert_fusion, f32[16,128,128]{1,2,0:T(8,128)} %get-tuple-element.26, f32[16,128]{1,0:T(8,128)S(1)} %get-tuple-element.25, bf16[256,256]{1,0:T(8,128)(2,1)S(1)} %copy-done.10), kind=kOutput, calls=%fused_computation.40 | convolution fusion | flops 404750336 | bytes 5382144 | tf_op jit(solution)/shard_map/axi,iy->axy/dot_general | solution.py:135
  (63 shorter events, 3.9 us)
Async XLA Ops:
  0.0 97.3 %copy-start = (bf16[256,768]{1,0:T(8,128)(2,1)S(1)}, bf16[256,768]{1,0:T(8,128)(2,1)}, u32[]{:S(2)}) copy-start(bf16[256,768]{1,0:T(8,128)(2,1)} %param.12) | copy-start | bytes 1179652
  0.0 3.7 %copy-start.1 = (bf16[4,16,32,256]{3,2,1,0:T(8,128)(2,1)S(1)}, bf16[4,16,32,256]{3,2,1,0:T(8,128)(2,1)}, u32[]{:S(2)}) copy-start(bf16[4,16,32,256]{3,2,1,0:T(8,128)(2,1)} %param.7) | copy-start | bytes 3145732
  0.0 5.7 %copy-start.2 = (bf16[256,2304]{1,0:T(8,128)(2,1)S(1)}, bf16[256,2304]{1,0:T(8,128)(2,1)}, u32[]{:S(2)}) copy-start(bf16[256,2304]{1,0:T(8,128)(2,1)} %param.10) | copy-start | bytes 3538948
  4.4 1.8 %collective-permute-start = (bf16[4,1,32,256]{3,2,1,0:T(8,128)(2,1)S(1)}, bf16[4,1,32,256]{3,2,1,0:T(8,128)(2,1)S(1)}, u32[]{:S(2)}, u32[]{:S(2)}) collective-permute-start(bf16[4,1,32,256]{3,2,1,0:T(8,128)(2,1)S(1)} %get-tuple-element.13), channel_id=1, source_target_pairs={} | collective-permute-start | bytes 196616 | tf_op jit(solution)/shard_map/ppermute | solution.py:21
  5.1 1.1 %collective-permute-start.1 = (bf16[4,1,32,256]{3,2,1,0:T(8,128)(2,1)S(1)}, bf16[4,1,32,256]{3,2,1,0:T(8,128)(2,1)S(1)}, u32[]{:S(2)}, u32[]{:S(2)}) collective-permute-start(bf16[4,1,32,256]{3,2,1,0:T(8,128)(2,1)S(1)} %get-tuple-element.14), channel_id=1, source_target_pairs={} | collective-permute-start | bytes 196616 | tf_op jit(solution)/shard_map/ppermute | solution.py:22
  6.3 2.2 %collective-permute-start.2 = (bf16[4,18,1,256]{3,2,1,0:T(2,128)(2,1)S(1)}, bf16[4,18,1,256]{3,2,1,0:T(2,128)(2,1)S(1)}, u32[]{:S(2)}, u32[]{:S(2)}) collective-permute-start(bf16[4,18,1,256]{3,2,1,0:T(2,128)(2,1)S(1)} %get-tuple-element.12), channel_id=1, source_target_pairs={} | collective-permute-start | bytes 110600 | tf_op jit(solution)/shard_map/ppermute | solution.py:21
  7.0 1.5 %collective-permute-start.3 = (bf16[4,18,1,256]{3,2,1,0:T(2,128)(2,1)S(1)}, bf16[4,18,1,256]{3,2,1,0:T(2,128)(2,1)S(1)}, u32[]{:S(2)}, u32[]{:S(2)}) collective-permute-start(bf16[4,18,1,256]{3,2,1,0:T(2,128)(2,1)S(1)} %get-tuple-element.11), channel_id=1, source_target_pairs={} | collective-permute-start | bytes 110600 | tf_op jit(solution)/shard_map/ppermute | solution.py:22
  11.7 4.6 %copy-start.9 = (s32[16]{0:T(128)S(1)}, s32[16]{0:T(128)}, u32[]{:S(2)}) copy-start(s32[16]{0:T(128)} %param.8) | copy-start | bytes 196
  13.8 4.2 %collective-permute-start.4 = (bf16[2,16,32,256]{3,2,1,0:T(8,128)(2,1)S(1)}, bf16[2,16,32,256]{3,2,1,0:T(8,128)(2,1)S(1)}, u32[]{:S(2)}, u32[]{:S(2)}) collective-permute-start(bf16[2,16,32,256]{3,2,1,0:T(8,128)(2,1)S(1)} %slice.154), channel_id=1, source_target_pairs={{0,1},{1,2},{2,3},{3,4},{4,5},{5,6},{6,7},{7,8},{8,9},{9,10},{10,1... | collective-permute-start | bytes 1572872 | tf_op jit(solution)/shard_map/ppermute | solution.py:30
  17.3 0.6 copy-start.7
  19.3 1.2 %copy-start.5 = (bf16[256,768]{1,0:T(8,128)(2,1)S(1)}, bf16[256,768]{1,0:T(8,128)(2,1)}, u32[]{:S(2)}) copy-start(bf16[256,768]{1,0:T(8,128)(2,1)} %param.11) | copy-start | bytes 1179652
  23.5 15.4 %copy-start.8 = (s32[128]{0:T(128)S(1)}, s32[128]{0:T(128)}, u32[]{:S(2)}) copy-start(s32[128]{0:T(128)} %copy-done.7) | copy-start | bytes 1540
  25.3 68.1 %all-to-all-start = ((bf16[4,512,256]{2,0,1:T(4,128)(2,1)}), bf16[4,512,256]{2,0,1:T(4,128)(2,1)S(1)}, u32[]{:S(2)}, u32[]{:S(2)}) async-start(bf16[4,512,256]{2,0,1:T(4,128)(2,1)} %copy.38), calls=%async_computation | async-start | bytes 2097152 | tf_op jit(solution)/shard_map/all_to_all | solution.py:111
  95.3 2.0 %copy-start.3 = (f32[128,256]{1,0:T(8,128)S(1)}, f32[128,256]{1,0:T(8,128)}, u32[]{:S(2)}) copy-start(f32[128,256]{1,0:T(8,128)} %copy.42) | copy-start | bytes 393220
  95.3 2.0 %copy-start.4 = (f32[128,256]{1,0:T(8,128)S(1)}, f32[128,256]{1,0:T(8,128)}, u32[]{:S(2)}) copy-start(f32[128,256]{1,0:T(8,128)} %copy.44) | copy-start | bytes 393220
  95.3 2.1 %copy-start.6 = (f32[1,256]{1,0:T(1,128)S(1)}, f32[1,256]{1,0:T(1,128)}, u32[]{:S(2)}) copy-start(f32[1,256]{1,0:T(1,128)} %get-tuple-element.17) | copy-start | bytes 3076
  100.0 3.1 %copy-start.10 = (bf16[256,256]{1,0:T(8,128)(2,1)S(1)}, bf16[256,256]{1,0:T(8,128)(2,1)}, u32[]{:S(2)}) copy-start(bf16[256,256]{1,0:T(8,128)(2,1)} %param.13) | copy-start | bytes 393220

commit v2 on v1

--- a/solution.py
+++ b/solution.py
@@ -3,6 +3,8 @@
 import jax
 import jax.numpy as jnp
 from jax import lax
+from jax.experimental import pallas as pl
+from jax.experimental.pallas import tpu as pltpu
 from jax.sharding import PartitionSpec as P
 
 GROUPS = 32
@@ -140,10 +142,338 @@
     )
     return mixed.reshape(1, 1, mixed.shape[0], total_frames, chans)
 
+HIGH = lax.Precision.HIGHEST
+VMEM_BYTES = 56 * 1024 * 1024
+
+
+def scalar_starts(lengths, first, count):
+    begins, at = [], jnp.int32(0)
+    for clip in range(lengths.shape[0]):
+        begins.append(at)
+        at = at + lengths[clip]
+    out = []
+    for i in range(count):
+        start = jnp.int32(0)
+        for begin in begins:
+            start = jnp.where(begin <= first + i, jnp.maximum(start, begin), start)
+        out.append(start)
+    return out
+
+
+def spread(rows, cols, of_row, of_col):
+    r = of_row(lax.broadcasted_iota(jnp.int32, (rows, cols), 0))
+    c = of_col(lax.broadcasted_iota(jnp.int32, (rows, cols), 1))
+    return jnp.where(r == c, 1.0, 0.0).astype(jnp.float32)
+
+
+def sum_rows(x):
+    return jnp.sum(x.reshape(x.shape[0] // 8, 8, x.shape[1]), axis=0)
+
+
+def front_kernel(n, lengths, video, gains, w_space, w_time, got, got_sums,
+                 act, ext, res, sums, ws, wt, w_sem, halo_sem, send_sem, recv_sem):
+    frames, height, width, chans = video.shape
+    pixels = height * width
+    per = pixels // n
+    half = frames // 2
+    gw = chans // GROUPS
+    me = lax.axis_index("tm")
+    barrier = pltpu.get_barrier_semaphore()
+
+    def greet(j, c):
+        pl.semaphore_signal(barrier, inc=1, device_id={"tm": lax.rem(me + j, n)},
+                            device_id_type=pl.DeviceIdType.MESH)
+        return c
+
+    lax.fori_loop(1, n, greet, 0)
+    loads = []
+    for tap in range(9):
+        loads.append(pltpu.make_async_copy(
+            w_space.at[:, pl.ds(tap * chans, chans)], ws.at[pl.ds(tap * chans, chans)], w_sem.at[tap]))
+    for tap in range(3):
+        loads.append(pltpu.make_async_copy(
+            w_time.at[:, pl.ds(tap * chans, chans)], wt.at[pl.ds(tap * chans, chans)], w_sem.at[9 + tap]))
+    for load in loads:
+        load.start()
+
+    group = spread(chans, chans, lambda r: r // gw, lambda c: c // gw)
+    rows = 4
+    step = rows * width
+    column = lax.rem(lax.broadcasted_iota(jnp.int32, (step, chans), 0), width)
+    gain = gains[0:1, :]
+    zero_row = jnp.zeros((1, width, 3 * chans), jnp.bfloat16)
+
+    def norm_act(f):
+        def moment(i, acc):
+            v = video[f, pl.ds(i * rows, rows)].reshape(step, chans).astype(jnp.float32)
+            return acc[0] + sum_rows(v), acc[1] + sum_rows(v * v)
+
+        zero = jnp.zeros((8, chans), jnp.float32)
+        total, square = lax.fori_loop(0, height // rows, moment, (zero, zero), unroll=True)
+        both = jnp.concatenate([total, square], axis=0)
+        both = lax.dot(both, group, precision=HIGH, preferred_element_type=jnp.float32)
+        count = pixels * gw
+        mean = jnp.sum(both[:8], axis=0, keepdims=True) / count
+        second = jnp.sum(both[8:], axis=0, keepdims=True) / count
+        scale = lax.rsqrt(second - mean * mean + EPS) * gain
+        act[f, 0:1] = zero_row
+        act[f, height + 1:height + 2] = zero_row
+
+        def put(i, c):
+            v = video[f, pl.ds(i * rows, rows)].reshape(step, chans).astype(jnp.float32)
+            v = (v - mean) * scale
+            v = v * (0.5 + 0.5 * jnp.tanh(0.5 * v))
+            left = jnp.where(column == 0, 0.0, pltpu.roll(v, 1, 0))
+            right = jnp.where(column == width - 1, 0.0, pltpu.roll(v, step - 1, 0))
+            for side, value in enumerate((left, v, right)):
+                act[f, pl.ds(1 + i * rows, rows), :, side * chans:(side + 1) * chans] = (
+                    value.astype(jnp.bfloat16).reshape(rows, width, chans))
+            return c
+
+        lax.fori_loop(0, height // rows, put, 0, unroll=True)
+
+    def conv(f):
+        total = None
+        for dy in range(3):
+            part = jnp.dot(act[f, dy:dy + height].reshape(pixels, 3 * chans),
+                           ws[dy * 3 * chans:(dy + 1) * 3 * chans],
+                           preferred_element_type=jnp.float32)
+            total = part if total is None else total + part
+        ext[2 + f] = total.astype(jnp.bfloat16)
+
+    halo = pltpu.make_async_remote_copy(
+        src_ref=ext.at[pl.ds(frames, 2)], dst_ref=ext.at[pl.ds(0, 2)],
+        send_sem=halo_sem.at[0], recv_sem=halo_sem.at[1],
+        device_id={"tm": lax.rem(me + 1, n)}, device_id_type=pl.DeviceIdType.MESH)
+
+    norm_act(2)
+    norm_act(3)
+    for load in loads:
+        load.wait()
+    conv(2)
+    conv(3)
+    pl.semaphore_wait(barrier, n - 1)
+
+    @pl.when(me < n - 1)
+    def _():
+        halo.start()
+
+    norm_act(0)
+    norm_act(1)
+    conv(0)
+    conv(1)
+
+    first = me * frames
+    starts = scalar_starts(lengths, first, frames)
+
+    def residual(f):
+        own, one, two = ext[2 + f], ext[1 + f], ext[f]
+        near = jnp.where(starts[f] <= first + f - 1, one, own)
+        far = jnp.where(starts[f] <= first + f - 2, two, near)
+        temporal = jnp.dot(jnp.concatenate([far, near, own], axis=1), wt[...],
+                           preferred_element_type=jnp.float32)
+        r = video[f].reshape(pixels, chans).astype(jnp.float32) + temporal
+        r = r.astype(jnp.bfloat16)
+        res[f // half, :, f % half] = r.reshape(n, per, chans)
+        r = r.astype(jnp.float32)
+        return sum_rows(r), sum_rows(r * r)
+
+    def send(part):
+        def one(j, c):
+            d = lax.rem(me + j, n)
+            pltpu.make_async_remote_copy(
+                src_ref=res.at[part, d], dst_ref=got.at[part, me],
+                send_sem=send_sem.at[part], recv_sem=recv_sem.at[part],
+                device_id={"tm": d}, device_id_type=pl.DeviceIdType.MESH).start()
+            return c
+
+        lax.fori_loop(1, n, one, 0)
+        pltpu.make_async_copy(res.at[part, me], got.at[part, me], recv_sem.at[part]).start()
+
+    stat = {}
+    stat[2] = residual(2)
+    stat[3] = residual(3)
+    send(1)
+
+    @pl.when(me > 0)
+    def _():
+        halo.wait_recv()
+
+    stat[0] = residual(0)
+    stat[1] = residual(1)
+    send(0)
+
+    low = spread(chans, 128, lambda r: r // gw, lambda c: c)
+    high = spread(chans, 128, lambda r: r // gw + GROUPS, lambda c: c)
+    total = jnp.concatenate([jnp.sum(stat[f][0], axis=0, keepdims=True) for f in range(frames)]
+                            + [jnp.zeros((8 - frames, chans), jnp.float32)], axis=0)
+    square = jnp.concatenate([jnp.sum(stat[f][1], axis=0, keepdims=True) for f in range(frames)]
+                             + [jnp.zeros((8 - frames, chans), jnp.float32)], axis=0)
+    sums[...] = (lax.dot(total, low, precision=HIGH, preferred_element_type=jnp.float32)
+                 + lax.dot(square, high, precision=HIGH, preferred_element_type=jnp.float32))
+
+    def tell(j, c):
+        pltpu.make_async_remote_copy(
+            src_ref=sums, dst_ref=got_sums.at[me], send_sem=send_sem.at[2], recv_sem=recv_sem.at[2],
+            device_id={"tm": lax.rem(me + j, n)}, device_id_type=pl.DeviceIdType.MESH).start()
+        return c
+
+    lax.fori_loop(1, n, tell, 0)
+    pltpu.make_async_copy(sums, got_sums.at[me], recv_sem.at[2]).start()
+
+    @pl.when(me < n - 1)
+    def _():
+        halo.wait_send()
+
+    for part in range(2):
+        pltpu.make_async_copy(got.at[part, pl.ds(0, n - 1)], got.at[part, pl.ds(0, n - 1)],
+                              send_sem.at[part]).wait()
+        pltpu.make_async_copy(got.at[part], got.at[part], recv_sem.at[part]).wait()
+    pltpu.make_async_copy(got_sums.at[pl.ds(0, n - 1)], got_sums.at[pl.ds(0, n - 1)],
+                          send_sem.at[2]).wait()
+    pltpu.make_async_copy(got_sums, got_sums, recv_sem.at[2]).wait()
+
+
+def front(n, lengths, video, gains, w_space, w_time):
+    frames, height, width, chans = video.shape
+    pixels = height * width
+    per = pixels // n
+    half = frames // 2
+    vmem = pl.BlockSpec(memory_space=pltpu.VMEM)
+    anyw = pl.BlockSpec(memory_space=pl.ANY)
+    bf16 = jnp.bfloat16
+    return pl.pallas_call(
+        lambda *refs: front_kernel(n, *refs),
+        out_shape=(jax.ShapeDtypeStruct((2, n, half, per, chans), bf16),
+                   jax.ShapeDtypeStruct((n, 8, 128), jnp.float32)),
+        in_specs=[pl.BlockSpec(memory_space=pltpu.SMEM), vmem, vmem, anyw, anyw],
+        out_specs=(anyw, anyw),
+        scratch_shapes=[
+            pltpu.VMEM((frames, height + 2, width, 3 * chans), bf16),
+            pltpu.VMEM((frames + 2, pixels, chans), bf16),
+            pltpu.VMEM((2, n, half, per, chans), bf16),
+            pltpu.VMEM((8, 128), jnp.float32),
+            pltpu.VMEM((9 * chans, chans), bf16),
+            pltpu.VMEM((3 * chans, chans), bf16),
+            pltpu.SemaphoreType.DMA((12,)),
+            pltpu.SemaphoreType.DMA((2,)),
+            pltpu.SemaphoreType.DMA((3,)),
+            pltpu.SemaphoreType.DMA((3,)),
+        ],
+        compiler_params=pltpu.CompilerParams(
+            collective_id=0, has_side_effects=True, vmem_limit_bytes=VMEM_BYTES),
+        cost_estimate=pl.CostEstimate(flops=3_300_000_000, bytes_accessed=4_000_000, transcendentals=600_000),
+        name="front",
+    )(lengths, video, gains, w_space, w_time)
+
+
+def tail_kernel(lengths, got, got_sums, gains, w_qkv, w_out, out, flat, mean, scale, open_):
+    _, n, half, per, chans = got.shape
+    frames = 2 * half
+    total = n * frames
+    gw = chans // GROUPS
+    count = out.shape[2]
+
+    @pl.when(pl.program_id(0) == 0)
+    def _():
+        block = 16
+        srcs = block // frames
+        side = block * per
+
+        def frame_of(r):
+            part, rest = r // (srcs * half * per), lax.rem(r, srcs * half * per)
+            src, rest = rest // (half * per), lax.rem(rest, half * per)
+            return src * frames + part * half + rest // per, lax.rem(rest, per)
+
+        def place(c):
+            f, p = frame_of(c)
+            return p * block + f
+
+        perm = spread(side, side, lambda r: r, place).astype(jnp.bfloat16)
+        for b in range(total // block):
+            x = jnp.concatenate(
+                [got[h, b * srcs:(b + 1) * srcs].reshape(srcs * half * per, chans) for h in range(2)], axis=0)
+            y = jnp.dot(perm, x, preferred_element_type=jnp.float32).astype(jnp.bfloat16)
+            flat[:, b * block:(b + 1) * block, :] = y.reshape(per, block, chans)
+        m = None
+        stats = got_sums[...].reshape(n * 8, 128)
+        pick = spread(total, n * 8, lambda r: r // frames * 8 + lax.rem(r, frames), lambda c: c)
+        stats = lax.dot(pick, stats, precision=HIGH, preferred_element_type=jnp.float32)
+        low = spread(128, chans, lambda r: r, lambda c: c // gw)
+        high = spread(128, chans, lambda r: r, lambda c: c // gw + GROUPS)
+        number = total_pixels(n, per) * gw
+        mu = lax.dot(stats, low, precision=HIGH, preferred_element_type=jnp.float32) / number
+        sq = lax.dot(stats, high, precision=HIGH, preferred_element_type=jnp.float32) / number
+        mean[...] = mu
+        scale[...] = lax.rsqrt(sq - mu * mu + EPS) * gains[1:2, :]
+        f = lax.broadcasted_iota(jnp.int32, (total, total), 0)
+        g = lax.broadcasted_iota(jnp.int32, (total, total), 1)
+        start = jnp.zeros((total, total), jnp.int32)
+        at = jnp.int32(0)
+        for clip in range(lengths.shape[0]):
+            start = jnp.where(at <= f, at, start)
+            at = at + lengths[clip]
+        open_[...] = jnp.where((g <= f) & (g >= start), 0.0, -1e30)
+
+    base = pl.program_id(0) * count
+    x = flat[pl.ds(base, count)]
+    normed = ((x.astype(jnp.float32) - mean[...][None]) * scale[...][None]).astype(jnp.bfloat16)
+    qkv = jnp.dot(normed.reshape(count * total, chans), w_qkv[...], preferred_element_type=jnp.float32)
+    query = (qkv[:, :chans] * (1.0 / math.sqrt(chans))).astype(jnp.bfloat16).reshape(count, total, chans)
+    keys = qkv[:, chans:2 * chans].astype(jnp.bfloat16).reshape(count, total, chans)
+    values = qkv[:, 2 * chans:].astype(jnp.bfloat16).reshape(count, total, chans)
+    shut = open_[...]
+    attn = []
+    for p in range(count):
+        score = lax.dot_general(query[p], keys[p], (((1,), (1,)), ((), ())),
+                                preferred_element_type=jnp.float32)
+        score = jnp.where(shut == 0.0, score, -1e30)
+        top = jnp.max(score, axis=1, keepdims=True)
+        expo = jnp.exp(score - top)
+        prob = (expo * (1.0 / jnp.sum(expo, axis=1, keepdims=True))).astype(jnp.bfloat16)
+        attn.append(jnp.dot(prob, values[p], preferred_element_type=jnp.float32).astype(jnp.bfloat16))
+    attn = jnp.concatenate(attn, axis=0)
+    proj = jnp.dot(attn, w_out[...], preferred_element_type=jnp.float32)
+    mixed = x.astype(jnp.float32) + proj.reshape(count, total, chans)
+    out[...] = mixed.astype(jnp.bfloat16).reshape(out.shape)
+
+
+def total_pixels(n, per):
+    return n * per
+
+
+def tail(lengths, got, got_sums, gains, w_qkv, w_out):
+    _, n, half, per, chans = got.shape
+    total = n * 2 * half
+    count = 4 if per % 4 == 0 else 1
+    vmem = pl.BlockSpec(memory_space=pltpu.VMEM)
+    return pl.pallas_call(
+        tail_kernel,
+        grid=(per // count,),
+        out_shape=jax.ShapeDtypeStruct((1, 1, per, total, chans), jnp.bfloat16),
+        in_specs=[pl.BlockSpec(memory_space=pltpu.SMEM), vmem, vmem, vmem, vmem, vmem],
+        out_specs=pl.BlockSpec((1, 1, count, total, chans), lambda i: (0, 0, i, 0, 0)),
+        scratch_shapes=[
+            pltpu.VMEM((per, total, chans), jnp.bfloat16),
+            pltpu.VMEM((total, chans), jnp.float32),
+            pltpu.VMEM((total, chans), jnp.float32),
+            pltpu.VMEM((total, total), jnp.float32),
+        ],
+        compiler_params=pltpu.CompilerParams(vmem_limit_bytes=VMEM_BYTES),
+        name="tail",
+    )(lengths, got, got_sums, gains, w_qkv, w_out)
+
+
+def whole_image(video, clip_lengths, norm_gains, spatial_kernel_weight, w_time, w_qkv, w_out):
+    n = lax.axis_size("tm")
+    got, got_sums = front(n, clip_lengths, video, norm_gains, spatial_kernel_weight, w_time)
+    return tail(clip_lengths, got, got_sums, norm_gains, w_qkv, w_out)
+
 
 def solution(mesh):
+    alone = mesh.shape["band"] * mesh.shape["fsdp"] == 1
     return jax.shard_map(
-        body,
+        whole_image if alone else body,
         mesh=mesh,
         in_specs=(
             P("tm", "band", "fsdp", None),

time: 107 us -> 47.4 us (0.44)
  blocking collectives: 52.2 us -> 0 us
  Pallas kernels: 0 us -> 47.1 us
  matrix products: 19.9 us -> 0 us
  starting transfers between devices: 18.8 us -> 0 us
  local copies, waits for them, and re-layouts: 8.25 us -> 0 us
  other arithmetic: 6.81 us -> 0 us
    all_gather x1 -> x0, blocking collectives: 52.2 us -> none  [body(): lax.all_gather(jnp.stack([mean_two, scale_two]), 'tm', axis=1, tiled=True)]
    pallas_call x0 -> x2, Pallas kernels: none -> 47.1 us  [the longest x1 38.8 us: front(): pl.pallas_call(lambda *refs: front_kernel(n, *refs), out_shape=(jax.Shape...]
    dot_general x17 -> x0, matrix products: 16.8 us -> none  [the longest x9 5.49 us: body(): jnp.einsum('fhwc,cd->fhwd', padded[:, shift_y:shift_y + height, shift_x:s...]
    all_to_all x1 -> x0, starting transfers between devices: 13.6 us -> none  [body(): lax.all_to_all(flat_resid, 'tm', split_axis=1, concat_axis=0, tiled=True)]
    ppermute x5 -> x0, starting transfers between devices: 5.21 us -> none  [the longest x1 2.58 us: from_behind(): return lax.ppermute(x, axis, pairs)]
    sub x1 -> x0, matrix products: 3.13 us -> none  [body(): expo = jnp.where(allowed[None], jnp.exp(scores - top), 0.0)]
    convert_element_type x2 -> x0, other arithmetic: 2.55 us -> none  [the longest x1 1.89 us: body(): jnp.swapaxes(resid_time, 0, 1).astype(jnp.float32) + projected_output]
    reduce_sum x5 -> x0, other arithmetic: 2.03 us -> none  [the longest x3 1.85 us: group_moments(): sums = jnp.sum(vals, axis=(1, 3))]
  transfers between devices with their start and end apart: 6 -> 0, of which waited for: 0 -> 0; matrix products, arithmetic and copies ran while one was open for 4% -> 0% of each run, Pallas kernels for 0% -> 0%
where the time goes in v2:
time: 47.4 us; the launch traced here: 47.1 us
  Pallas kernels  47.1 us (99%)
    pallas_call x1, Pallas kernels, front(): pl.pallas_call(lambda *refs: front_kernel(n, *refs), out_shape=(jax.Shape...  38.8 us
    pallas_call x1, Pallas kernels, tail(): pl.pallas_call(tail_kernel, grid=(per // count,), out_shape=jax.ShapeDtyp...  8.3 us

profile of v2, /device:TPU:0, one launch (start us, length us, event | category | flops | bytes accessed | tf_op | source)
XLA Modules:
  0.0 47.1 jit_solution(15878169683143906748)
XLA Ops:
  0.0 38.8 %front.1 = (bf16[2,32,2,16,256]{4,3,2,1,0:T(8,128)(2,1)}, f32[32,8,128]{2,1,0:T(8,128)}) custom-call(s32[16]{0:T(128)} %lengths.1, bf16[4,16,32,256]{3,2,1,0:T(8,128)(2,1)} %refs_1_.1, f32[2,256]{1,0:T(2,128)} %gains.1, bf16[256,2304]{1,0:T(8,128)(2,1)} %refs_3_.1, bf16[256,768]{1,0:T(8,128)(2,1)} %refs_4_.1), custom_call_target="tpu_custom_call" | custom-call | flops 3300000000 | bytes 4000000 | tf_op jit(solution)/shard_map/front/pallas_call | solution.py:345
  38.8 8.3 %tail.1 = bf16[1,1,16,128,256]{4,3,2,1,0:T(8,128)(2,1)} custom-call(s32[16]{0:T(128)} %lengths.1, bf16[2,32,2,16,256]{4,3,2,1,0:T(8,128)(2,1)} %get-tuple-element.7.got, f32[32,8,128]{2,1,0:T(8,128)} %get-tuple-element.8.got_sums, f32[2,256]{1,0:T(2,128)} %gains.1, bf16[256,768]{1,0:T(8,128)(2,1)} %w_qkv.1, bf16[256,256]{1,0:T(8,128)(2,1)} %w_out.1), custom_call_target="tpu_custom_call" | custom-call | tf_op jit(solution)/shard_map/tail/pallas_call | solution.py:450

commit v3 on v1

--- a/solution.py
+++ b/solution.py
@@ -3,6 +3,8 @@
 import jax
 import jax.numpy as jnp
 from jax import lax
+from jax.experimental import pallas as pl
+from jax.experimental.pallas import tpu as pltpu
 from jax.sharding import PartitionSpec as P
 
 GROUPS = 32
@@ -140,10 +142,331 @@
     )
     return mixed.reshape(1, 1, mixed.shape[0], total_frames, chans)
 
+HIGH = lax.Precision.HIGHEST
+VMEM_BYTES = 56 * 1024 * 1024
+
+
+def scalar_starts(lengths, first, count):
+    begins, at = [], jnp.int32(0)
+    for clip in range(lengths.shape[0]):
+        begins.append(at)
+        at = at + lengths[clip]
+    out = []
+    for i in range(count):
+        start = jnp.int32(0)
+        for begin in begins:
+            start = jnp.where(begin <= first + i, jnp.maximum(start, begin), start)
+        out.append(start)
+    return out
+
+
+def over(x, k):
+    return x >> (k.bit_length() - 1) if k & (k - 1) == 0 else x // k
+
+
+def left_of(x, k):
+    return x & (k - 1) if k & (k - 1) == 0 else lax.rem(x, k)
+
+
+def spread(rows, cols, of_row, of_col):
+    r = of_row(lax.broadcasted_iota(jnp.int32, (rows, cols), 0))
+    c = of_col(lax.broadcasted_iota(jnp.int32, (rows, cols), 1))
+    return jnp.where(r == c, 1.0, 0.0).astype(jnp.float32)
+
+
+def exact_dot(a, b):
+    return lax.dot(a, b, precision=HIGH, preferred_element_type=jnp.float32)
+
+
+def sum_rows(x):
+    return jnp.sum(x.reshape(x.shape[0] // 8, 8, x.shape[1]), axis=0)
+
+
+def kernel(n, lengths, video, gains, w_space, w_time, w_qkv, w_out, out,
+           before, act, ext, res_a, res_b, got_a, got_b, sums, got_sums, ws, wt, flat, done,
+           mean_all, scale_all, shut, w_sem, halo_sem, send_sem, recv_sem, out_sem):
+    frames, height, width, chans = video.shape
+    pixels = height * width
+    per = pixels // n
+    part_px = per // 2
+    gw = chans // GROUPS
+    total = n * frames
+    me = lax.axis_index("tm")
+    barrier = pltpu.get_barrier_semaphore()
+
+    def greet(j, c):
+        pl.semaphore_signal(barrier, inc=1, device_id={"tm": lax.rem(me + j, n)},
+                            device_id_type=pl.DeviceIdType.MESH)
+        return c
+
+    lax.fori_loop(1, n, greet, 0)
+    loads = []
+    for tap in range(9):
+        loads.append(pltpu.make_async_copy(
+            w_space.at[:, pl.ds(tap * chans, chans)], ws.at[pl.ds(tap * chans, chans)], w_sem.at[tap]))
+    for tap in range(3):
+        loads.append(pltpu.make_async_copy(
+            w_time.at[:, pl.ds(tap * chans, chans)], wt.at[pl.ds(tap * chans, chans)], w_sem.at[9 + tap]))
+    for load in loads:
+        load.start()
+
+    group = spread(chans, chans, lambda r: over(r, gw), lambda c: over(c, gw))
+    rows = 4
+    step = rows * width
+    column = left_of(lax.broadcasted_iota(jnp.int32, (step, chans), 0), width)
+    gain = gains[0:1, :]
+    zero_row = jnp.zeros((1, width, 3 * chans), jnp.bfloat16)
+
+    def norm_act(source, f, slot):
+        def moment(i, acc):
+            v = source[f, pl.ds(i * rows, rows)].reshape(step, chans).astype(jnp.float32)
+            return acc[0] + sum_rows(v), acc[1] + sum_rows(v * v)
+
+        zero = jnp.zeros((8, chans), jnp.float32)
+        one, two = lax.fori_loop(0, height // rows, moment, (zero, zero), unroll=True)
+        both = exact_dot(jnp.concatenate([one, two], axis=0), group)
+        count = pixels * gw
+        mean = jnp.sum(both[:8], axis=0, keepdims=True) / count
+        second = jnp.sum(both[8:], axis=0, keepdims=True) / count
+        scale = lax.rsqrt(second - mean * mean + EPS) * gain
+        act[slot, 0:1] = zero_row
+        act[slot, height + 1:height + 2] = zero_row
+
+        def put(i, c):
+            v = source[f, pl.ds(i * rows, rows)].reshape(step, chans).astype(jnp.float32)
+            v = (v - mean) * scale
+            v = v * (0.5 + 0.5 * jnp.tanh(0.5 * v))
+            left = jnp.where(column == 0, 0.0, pltpu.roll(v, 1, 0))
+            right = jnp.where(column == width - 1, 0.0, pltpu.roll(v, step - 1, 0))
+            for side, value in enumerate((left, v, right)):
+                act[slot, pl.ds(1 + i * rows, rows), :, side * chans:(side + 1) * chans] = (
+                    value.astype(jnp.bfloat16).reshape(rows, width, chans))
+            return c
+
+        lax.fori_loop(0, height // rows, put, 0, unroll=True)
+
+    def conv(slot, to):
+        acc = None
+        for dy in range(3):
+            part = jnp.dot(act[slot, dy:dy + height].reshape(pixels, 3 * chans),
+                           ws[dy * 3 * chans:(dy + 1) * 3 * chans],
+                           preferred_element_type=jnp.float32)
+            acc = part if acc is None else acc + part
+        ext[to] = acc.astype(jnp.bfloat16)
+
+    halo = pltpu.make_async_remote_copy(
+        src_ref=video.at[pl.ds(frames - 2, 2)], dst_ref=before,
+        send_sem=halo_sem.at[0], recv_sem=halo_sem.at[1],
+        device_id={"tm": lax.rem(me + 1, n)}, device_id_type=pl.DeviceIdType.MESH)
+
+    norm_act(video, 0, 0)
+    pl.semaphore_wait(barrier, n - 1)
+
+    @pl.when(me < n - 1)
+    def _():
+        halo.start()
+
+    for f in range(1, frames):
+        norm_act(video, f, f)
+    for load in loads:
+        load.wait()
+    for f in range(frames):
+        conv(f, 2 + f)
+
+    first = me * frames
+    starts = scalar_starts(lengths, first, frames)
+    stat = {}
+
+    def residual(f):
+        own, one, two = ext[2 + f], ext[1 + f], ext[f]
+        near = jnp.where(starts[f] <= first + f - 1, one, own)
+        far = jnp.where(starts[f] <= first + f - 2, two, near)
+        temporal = jnp.dot(jnp.concatenate([far, near, own], axis=1), wt[...],
+                           preferred_element_type=jnp.float32)
+        r = video[f].reshape(pixels, chans).astype(jnp.float32) + temporal
+        r = r.astype(jnp.bfloat16).astype(jnp.float32)
+        stat[f] = jnp.concatenate([sum_rows(r), sum_rows(r * r)], axis=0)
+        return r.reshape(n, 2, part_px, chans)
+
+    def pair(part):
+        r = [residual(2 * part + i) for i in range(2)]
+        res_a[part] = jnp.concatenate([r[0][:, 0], r[1][:, 0]], axis=1).astype(jnp.bfloat16)
+        res_b[:, 2 * part * part_px:2 * (part + 1) * part_px] = (
+            jnp.concatenate([r[0][:, 1], r[1][:, 1]], axis=1).astype(jnp.bfloat16))
+
+    def exchange(source, target, which, picked):
+        def one(j, c):
+            d = lax.rem(me + j, n)
+            pltpu.make_async_remote_copy(
+                src_ref=source.at[d] if picked else source, dst_ref=target.at[me],
+                send_sem=send_sem.at[which], recv_sem=recv_sem.at[which],
+                device_id={"tm": d}, device_id_type=pl.DeviceIdType.MESH).start()
+            return c
+
+        lax.fori_loop(1, n, one, 0)
+        pltpu.make_async_copy(source.at[me] if picked else source, target.at[me],
+                              recv_sem.at[which]).start()
+
+    pair(1)
+    exchange(res_a.at[1], got_a.at[1], 1, True)
+
+    @pl.when(me > 0)
+    def _():
+        halo.wait_recv()
+
+    for i in range(2):
+        norm_act(before, i, i)
+    for i in range(2):
+        conv(i, i)
+    pair(0)
+    exchange(res_a.at[0], got_a.at[0], 0, True)
+    pack = None
+    for f in range(frames):
+        put_at = spread(chans, 128, lambda r: over(r, gw) + f * GROUPS, lambda c: c)
+        term = exact_dot(stat[f], put_at)
+        pack = term if pack is None else pack + term
+    sums[0:1] = jnp.sum(pack[:8], axis=0, keepdims=True)
+    sums[1:2] = jnp.sum(pack[8:], axis=0, keepdims=True)
+    exchange(sums, got_sums, 2, False)
+    exchange(res_b, got_b, 3, True)
+
+    block = 32
+    srcs = block // frames
+    side = block * part_px
+    group_rows = srcs * 2 * part_px
+
+    def place(c):
+        part, rest = over(c, group_rows), left_of(c, group_rows)
+        src, rest = over(rest, 2 * part_px), left_of(rest, 2 * part_px)
+        f = src * frames + part * 2 + over(rest, part_px)
+        return left_of(rest, part_px) * block + f
+
+    perm = spread(side, side, lambda r: r, place).astype(jnp.bfloat16)
+    f_at = lax.broadcasted_iota(jnp.int32, (total, total), 0)
+    g_at = lax.broadcasted_iota(jnp.int32, (total, total), 1)
+    start = jnp.zeros((total, total), jnp.int32)
+    at = jnp.int32(0)
+    for clip in range(lengths.shape[0]):
+        start = jnp.where(at <= f_at, at, start)
+        at = at + lengths[clip]
+    shut[...] = jnp.where((g_at <= f_at) & (g_at >= start), 0.0, 1.0)
+
+    pltpu.make_async_copy(got_sums, got_sums, recv_sem.at[2]).wait()
+    pick = spread(total, n, lambda r: over(r, frames), lambda c: c)
+    lane = spread(total, 128, lambda r: left_of(r, frames), lambda c: over(c, GROUPS))
+    wide = spread(128, chans, lambda r: left_of(r, GROUPS), lambda c: over(c, gw))
+    count = pixels * gw
+    mu = exact_dot(exact_dot(pick, got_sums[:, 0, :]) * lane, wide) / count
+    sq = exact_dot(exact_dot(pick, got_sums[:, 1, :]) * lane, wide) / count
+    mean_all[...] = mu
+    scale_all[...] = lax.rsqrt(sq - mu * mu + EPS) * gains[1:2, :]
+
+    def attend(at_px, number):
+        x = flat[pl.ds(at_px, number)]
+        normed = ((x.astype(jnp.float32) - mean_all[...][None]) * scale_all[...][None]).astype(jnp.bfloat16)
+        qkv = jnp.dot(normed.reshape(number * total, chans), w_qkv[...], preferred_element_type=jnp.float32)
+        query = (qkv[:, :chans] * (1.0 / math.sqrt(chans))).astype(jnp.bfloat16).reshape(number, total, chans)
+        keys = qkv[:, chans:2 * chans].astype(jnp.bfloat16).reshape(number, total, chans)
+        values = qkv[:, 2 * chans:].astype(jnp.bfloat16).reshape(number, total, chans)
+        closed = shut[...] > 0.5
+        probs = []
+        for p in range(number):
+            score = lax.dot_general(query[p], keys[p], (((1,), (1,)), ((), ())),
+                                    preferred_element_type=jnp.float32)
+            score = jnp.where(closed, -1e30, score)
+            top = jnp.max(score, axis=1, keepdims=True)
+            expo = jnp.exp(score - top)
+            probs.append((expo * (1.0 / jnp.sum(expo, axis=1, keepdims=True))).astype(jnp.bfloat16))
+        attn = jnp.concatenate(
+            [jnp.dot(probs[p], values[p], preferred_element_type=jnp.float32).astype(jnp.bfloat16)
+             for p in range(number)], axis=0)
+        proj = jnp.dot(attn, w_out[...], preferred_element_type=jnp.float32)
+        mixed = x.astype(jnp.float32) + proj.reshape(number, total, chans)
+        done[pl.ds(at_px, number)] = mixed.astype(jnp.bfloat16)
+        store = pltpu.make_async_copy(done.at[pl.ds(at_px, number)], out.at[0, 0, pl.ds(at_px, number)],
+                                      out_sem.at[at_px // number])
+        store.start()
+        return store
+
+    def regroup(at_px, piece):
+        for b in range(total // block):
+            x = jnp.concatenate([piece(p, b * srcs, (b + 1) * srcs) for p in range(2)], axis=0)
+            y = jnp.dot(perm, x, preferred_element_type=jnp.float32).astype(jnp.bfloat16)
+            flat[at_px:at_px + part_px, b * block:(b + 1) * block, :] = y.reshape(part_px, block, chans)
+
+    stores = []
+    number = part_px // 2
+    for part in range(2):
+        pltpu.make_async_copy(got_a.at[part], got_a.at[part], recv_sem.at[part]).wait()
+    regroup(0, lambda p, lo, hi: got_a[p, lo:hi].reshape(group_rows, chans))
+    for i in range(2):
+        stores.append(attend(i * number, number))
+    pltpu.make_async_copy(got_b, got_b, recv_sem.at[3]).wait()
+    regroup(part_px, lambda p, lo, hi: got_b[lo:hi, p * 2 * part_px:(p + 1) * 2 * part_px].reshape(group_rows, chans))
+    for i in range(2):
+        stores.append(attend(part_px + i * number, number))
+
+    @pl.when(me < n - 1)
+    def _():
+        halo.wait_send()
+
+    for part in range(2):
+        pltpu.make_async_copy(got_a.at[part, pl.ds(0, n - 1)], got_a.at[part, pl.ds(0, n - 1)],
+                              send_sem.at[part]).wait()
+    pltpu.make_async_copy(got_sums.at[pl.ds(0, n - 1)], got_sums.at[pl.ds(0, n - 1)], send_sem.at[2]).wait()
+    pltpu.make_async_copy(got_b.at[pl.ds(0, n - 1)], got_b.at[pl.ds(0, n - 1)], send_sem.at[3]).wait()
+    for store in stores:
+        store.wait()
+
+
+def whole_image(video, clip_lengths, norm_gains, spatial_kernel_weight, w_time, w_qkv, w_out):
+    n = lax.axis_size("tm")
+    frames, height, width, chans = video.shape
+    pixels = height * width
+    per = pixels // n
+    total = n * frames
+    vmem = pl.BlockSpec(memory_space=pltpu.VMEM)
+    anyw = pl.BlockSpec(memory_space=pl.ANY)
+    bf16 = jnp.bfloat16
+    return pl.pallas_call(
+        lambda *refs: kernel(n, *refs),
+        out_shape=jax.ShapeDtypeStruct((1, 1, per, total, chans), bf16),
+        in_specs=[pl.BlockSpec(memory_space=pltpu.SMEM), vmem, vmem, anyw, anyw, vmem, vmem],
+        out_specs=anyw,
+        scratch_shapes=[
+            pltpu.VMEM((2, height, width, chans), bf16),
+            pltpu.VMEM((frames, height + 2, width, 3 * chans), bf16),
+            pltpu.VMEM((frames + 2, pixels, chans), bf16),
+            pltpu.VMEM((2, n, per, chans), bf16),
+            pltpu.VMEM((n, 2 * per, chans), bf16),
+            pltpu.VMEM((2, n, per, chans), bf16),
+            pltpu.VMEM((n, 2 * per, chans), bf16),
+            pltpu.VMEM((2, 128), jnp.float32),
+            pltpu.VMEM((n, 2, 128), jnp.float32),
+            pltpu.VMEM((9 * chans, chans), bf16),
+            pltpu.VMEM((3 * chans, chans), bf16),
+            pltpu.VMEM((per, total, chans), bf16),
+            pltpu.VMEM((per, total, chans), bf16),
+            pltpu.VMEM((total, chans), jnp.float32),
+            pltpu.VMEM((total, chans), jnp.float32),
+            pltpu.VMEM((total, total), jnp.float32),
+            pltpu.SemaphoreType.DMA((12,)),
+            pltpu.SemaphoreType.DMA((2,)),
+            pltpu.SemaphoreType.DMA((4,)),
+            pltpu.SemaphoreType.DMA((4,)),
+            pltpu.SemaphoreType.DMA((4,)),
+        ],
+        compiler_params=pltpu.CompilerParams(
+            collective_id=0, has_side_effects=True, vmem_limit_bytes=VMEM_BYTES),
+        cost_estimate=pl.CostEstimate(flops=5_000_000_000, bytes_accessed=4_000_000, transcendentals=900_000),
+        name="block",
+    )(clip_lengths, video, norm_gains, spatial_kernel_weight, w_time, w_qkv, w_out)
+
 
 def solution(mesh):
+    alone = mesh.shape["band"] * mesh.shape["fsdp"] == 1
     return jax.shard_map(
-        body,
+        whole_image if alone else body,
         mesh=mesh,
         in_specs=(
             P("tm", "band", "fsdp", None),

time: 107 us -> 40.8 us (0.38)
  blocking collectives: 52.2 us -> 0 us
  Pallas kernels: 0 us -> 37.7 us
  matrix products: 19.9 us -> 0 us
  starting transfers between devices: 18.8 us -> 0 us
  other arithmetic: 6.81 us -> 0 us
  local copies, waits for them, and re-layouts: 8.25 us -> 2.29 us
    all_gather x1 -> x0, blocking collectives: 52.2 us -> none  [body(): lax.all_gather(jnp.stack([mean_two, scale_two]), 'tm', axis=1, tiled=True)]
    pallas_call x0 -> x1, Pallas kernels: none -> 37.7 us  [whole_image(): pl.pallas_call(lambda *refs: kernel(n, *refs), out_shape=jax.ShapeDtypeSt...]
    dot_general x17 -> x0, matrix products: 16.8 us -> none  [the longest x9 5.49 us: body(): jnp.einsum('fhwc,cd->fhwd', padded[:, shift_y:shift_y + height, shift_x:s...]
    all_to_all x1 -> x0, starting transfers between devices: 13.6 us -> none  [body(): lax.all_to_all(flat_resid, 'tm', split_axis=1, concat_axis=0, tiled=True)]
    ppermute x5 -> x0, starting transfers between devices: 5.21 us -> none  [the longest x1 2.58 us: from_behind(): return lax.ppermute(x, axis, pairs)]
    sub x1 -> x0, matrix products: 3.13 us -> none  [body(): expo = jnp.where(allowed[None], jnp.exp(scores - top), 0.0)]
    convert_element_type x2 -> x0, other arithmetic: 2.55 us -> none  [the longest x1 1.89 us: body(): jnp.swapaxes(resid_time, 0, 1).astype(jnp.float32) + projected_output]
    reduce_sum x5 -> x0, other arithmetic: 2.03 us -> none  [the longest x3 1.85 us: group_moments(): sums = jnp.sum(vals, axis=(1, 3))]
  transfers between devices with their start and end apart: 6 -> 0, of which waited for: 0 -> 0; matrix products, arithmetic and copies ran while one was open for 4% -> 0% of each run, Pallas kernels for 0% -> 0%
where the time goes in v3:
time: 40.8 us; the launch traced here: 40 us
  Pallas kernels  37.7 us (92%)
  local copies, waits for them, and re-layouts  2.29 us (6%)
    pallas_call x1, Pallas kernels, whole_image(): pl.pallas_call(lambda *refs: kernel(n, *refs), out_shape=jax.ShapeDtypeSt...  37.7 us
    unnamed x1, local copies, waits for them, and re-layouts  2.29 us

profile of v3, /device:TPU:0, one launch (start us, length us, event | category | flops | bytes accessed | tf_op | source)
XLA Modules:
  0.0 40.0 jit_solution(9402330357742128009)
XLA Ops:
  0.0 37.7 %block.1 = bf16[1,1,16,128,256]{4,3,2,1,0:T(8,128)(2,1)} custom-call(s32[16]{0:T(128)} %refs_0_.1, bf16[4,16,32,256]{3,2,1,0:T(8,128)(2,1)} %refs_1_.1, f32[2,256]{1,0:T(2,128)} %refs_2_.1, bf16[256,2304]{1,0:T(8,128)(2,1)} %refs_3_.1, bf16[256,768]{1,0:T(8,128)(2,1)} %refs_4_.1, bf16[256,768]{1,0:T(8,128)(2,1)} %refs_5_.1, bf16[256,256]{1,0:T(8,128)(2,1)} %refs_6_.1), custom_call_target="tpu_custom_call" | custom-call | flops 5000000000 | bytes 4000000 | tf_op jit(solution)/shard_map/block/pallas_call | solution.py:431
  37.7 2.3 %copy.9 = bf16[1,1,16,128,256]{4,3,2,1,0:T(8,128)(2,1)} copy(bf16[1,1,16,128,256]{4,3,2,1,0:T(8,128)(2,1)} %block.1) | data formatting | bytes 2097152
